TPU v7x, 256 devices: a whole 4x4x8 slice. The times are simulated.
256 devices in a mesh: gx: 16 (over z, core), gy: 16 (over x, y).
Axes of the slice: x: 4, y: 4, z: 8, core: 2. Of those that a mesh axis runs over, the one named last changes fastest.
Arguments:
- velocity: float32 [3, 8192, 8192], P(None, 'gx', 'gy'), may hold values from -6 to 6
- metric_first: float32 [8192], P('gy'), may hold values from 0.5 to 2
- metric_second: float32 [8192], P('gy'), may hold values from -4 to 4
Outputs:
- increment: float32 [3, 8192, 8192], P(None, 'gx', 'gy')
All inputs are finite; a program needn't handle non-finite values.
Results may differ from a plain program's by a relative error of at most 0.0003.
Values sent between devices are 32-bit elements; how exact they have to be, the bound alone decides.
No kernel may reach another device: no remote copies, remote signals or barrier semaphores. Data moves between devices by JAX's collectives and lax.ppermute only.
A program may use at most 128 MiB of HBM per device.

v0:
```python
import math
import jax
import jax.numpy as jnp
import numpy as np
from jax import lax
from jax.sharding import PartitionSpec as P

VISCOSITY = 0.2
DIFFUSION = 1.0
HIGHEST = lax.Precision.HIGHEST


def extended(cells, sides, width, closed):
    for axis, dim in sides:
        count = lax.axis_size(axis)
        ends = count if closed else count - 1
        head = lax.slice_in_dim(cells, 0, width, axis=dim)
        tail = lax.slice_in_dim(cells, cells.shape[dim] - width, cells.shape[dim], axis=dim)
        cells = jnp.concatenate(
            [
                lax.ppermute(tail, axis, [(i, (i + 1) % count) for i in range(ends)]),
                cells,
                lax.ppermute(head, axis, [((i + 1) % count, i) for i in range(ends)]),
            ],
            axis=dim,
        )
    return cells


def stencils(field, ahead):
    first_rhs = (
        45.0 * (ahead(1) - ahead(-1)) - 9.0 * (ahead(2) - ahead(-2)) + (ahead(3) - ahead(-3))
    ) / 60.0
    second_rhs = (
        270.0 * (ahead(1) + ahead(-1))
        - 27.0 * (ahead(2) + ahead(-2))
        + 2.0 * (ahead(3) + ahead(-3))
        - 490.0 * field
    ) / 180.0
    return (first_rhs, second_rhs)


def coefficients(cells):
    sigma = cells / 4.0
    diag = 1.0 + 2.0 * DIFFUSION + sigma
    return (-(DIFFUSION + sigma) / diag, -DIFFUSION / diag, diag, sigma)


def invert(matrix):
    order = matrix.shape[0]
    augmented = np.concatenate([matrix, np.eye(order)], axis=1)
    for pivot in range(order):
        augmented[pivot] = augmented[pivot] / augmented[pivot, pivot]
        column_k = augmented[:, pivot].copy()
        column_k[pivot] = 0.0
        augmented = augmented - np.outer(column_k, augmented[pivot])
    return augmented[:, order:]


def band_matrix(below, main, above, periodic):
    order = main.shape[0]
    matrix = np.eye(order) * main
    for row_at in range(1, order):
        matrix[row_at, row_at - 1] = below[row_at]
    for row_at in range(order - 1):
        matrix[row_at, row_at + 1] = above[row_at]
    if periodic:
        matrix[0, order - 1] = matrix[0, order - 1] + below[0]
        matrix[order - 1, 0] = matrix[order - 1, 0] + above[order - 1]
    return matrix


def block_parts(length, lower, upper):
    inner_len = length - 2
    ones = np.ones((inner_len,))
    inverse = invert(band_matrix(lower * ones, ones, upper * ones, False))
    head_col = -lower * inverse[:, 0]
    tail_col = -upper * inverse[:, -1]
    return (inverse, head_col, tail_col)


def reduced_inverse(blocks, lower, upper, head_col, tail_col, periodic):
    order_two = 2 * blocks
    is_even = np.arange(order_two) % 2 == 0
    below = np.where(is_even, lower, lower * head_col[-1])
    main = np.where(is_even, 1.0 + upper * head_col[0], 1.0 + lower * tail_col[-1])
    above = np.where(is_even, upper * tail_col[0], upper)
    return invert(band_matrix(below, main, above, periodic))


def constants(length, lower, upper, blocks, own_block, periodic):
    inverse, head_col, tail_col = block_parts(length, lower, upper)
    reduced = reduced_inverse(blocks, lower, upper, head_col, tail_col, periodic)
    own_rows = lax.dynamic_slice_in_dim(jnp.asarray(reduced, jnp.float32), 2 * own_block, 2, 0)
    return (
        jnp.asarray(inverse, jnp.float32),
        jnp.asarray(head_col, jnp.float32),
        jnp.asarray(tail_col, jnp.float32),
        own_rows,
    )


def make_fold(own_rows, total, piece):
    span_len = piece.shape[1]
    rows_used = lax.slice_in_dim(own_rows, 0, span_len, axis=1)
    return total + jnp.einsum("ij,cjl->cil", rows_used, piece, precision=HIGHEST)


def partitioned_x(right_side, lower, upper):
    inverse, head_col, tail_col, own_rows = constants(
        right_side.shape[1], lower, upper, lax.axis_size("gx"), lax.axis_index("gx"), True
    )
    interior = jnp.einsum("cjy,ij->ciy", right_side[:, 1:-1, :], inverse, precision=HIGHEST)
    head_val = right_side[:, 0, :] - upper * interior[:, 0, :]
    tail_val = right_side[:, -1, :] - lower * interior[:, -1, :]
    ends = jnp.stack([head_val, tail_val], axis=1)
    solved = make_fold(
        own_rows, jnp.zeros(ends.shape, jnp.float32), lax.all_gather(ends, "gx", axis=1, tiled=True)
    )
    head_x = solved[:, 0:1, :]
    tail_x = solved[:, 1:2, :]
    middle = interior + head_col[None, :, None] * head_x + tail_col[None, :, None] * tail_x
    return jnp.concatenate([head_x, middle, tail_x], axis=1)


def local(velocity, metric_first, metric_second):
    cells_x = velocity.shape[1]
    cells_y = velocity.shape[2]
    low_x, up_x, diag_x, sig_x = coefficients(lax.axis_size("gx") * cells_x)
    low_y, up_y, diag_y, sig_y = coefficients(lax.axis_size("gy") * cells_y)
    x_padded = extended(velocity, (("gx", 1),), 3, True)
    y_padded = extended(velocity, (("gy", 2),), 3, False)
    first_x, second_x = stencils(
        velocity, lambda steps: x_padded[:, 3 + steps : 3 + steps + cells_x, :]
    )
    first_eta, second_eta = stencils(
        velocity, lambda steps: y_padded[:, :, 3 + steps : 3 + steps + cells_y]
    )
    slope_y = metric_first * first_eta
    curve_y = metric_first * metric_first * second_eta + metric_second * first_eta
    tendency = -(velocity[0:1] * first_x + velocity[1:2] * slope_y) + VISCOSITY * (
        second_x + curve_y
    )
    right_side = tendency * (math.sqrt(sig_x * sig_y) / diag_x)
    half = partitioned_x(right_side, low_x, up_x)
    y_lines = half / diag_y
    inverse, head_col, tail_col, own_rows = constants(
        cells_y, low_y, up_y, lax.axis_size("gy"), lax.axis_index("gy"), False
    )
    interior = jnp.einsum("cxj,ij->cxi", y_lines[..., 1:-1], inverse, precision=HIGHEST)
    head_val = y_lines[..., 0] - up_y * interior[..., 0]
    tail_val = y_lines[..., -1] - low_y * interior[..., -1]
    ends = jnp.stack([head_val, tail_val], axis=1)
    solved = make_fold(
        own_rows, jnp.zeros(ends.shape, jnp.float32), lax.all_gather(ends, "gy", axis=1, tiled=True)
    )
    head_y = solved[:, 0][..., None]
    tail_y = solved[:, 1][..., None]
    middle = interior + head_col * head_y + tail_col * tail_y
    return jnp.concatenate([head_y, middle, tail_y], axis=-1)


def solution(mesh):
    in_specs = (P(None, "gx", "gy"), P("gy"), P("gy"))
    out_specs = P(None, "gx", "gy")
    return jax.shard_map(local, mesh=mesh, in_specs=in_specs, out_specs=out_specs, check_vma=False)
```

profile of v0, /device:TPU:32, one launch (start us, length us, event | category | flops | bytes accessed | tf_op | source)
XLA Modules:
  0.0 107.2 jit_solution(8872015902211756143)
XLA Ops:
  0.0 0.0 copy-start
  0.0 1.0 fusion.26
  1.0 0.0 collective-permute-start
  1.0 2.8 %fusion.27 = (f32[3,512,3]{2,1,0:T(8,128)}, f32[3,512,3]{2,1,0:T(8,128)}) fusion(f32[3,512,512]{2,1,0:T(8,128)} %param.11), kind=kLoop, calls=%fused_computation.64 | loop fusion | bytes 73728 | tf_op jit(solution)/shard_map/slice | solution.py:18
  3.8 0.0 copy-start.7
  3.8 0.0 copy-start.8
  3.8 1.4 %copy.40 = f32[3,512,3]{1,2,0:T(4,128)S(1)} copy(f32[3,512,3]{2,1,0:T(8,128)} %get-tuple-element.16) | data formatting | bytes 36864
  5.2 1.3 %collective-permute-start.2 = (f32[3,512,3]{1,2,0:T(4,128)S(1)}, f32[3,512,3]{1,2,0:T(4,128)S(1)}, u32[]{:S(2)}, u32[]{:S(2)}) collective-permute-start(f32[3,512,3]{1,2,0:T(4,128)S(1)} %copy.40), channel_id=1, source_target_pairs={{1,0},{2,1},{3,2},{4,3},{5,4},{6,5},{7,6},{8,7},{9,8},{10,9},{11,1... | collective-permute-start | bytes 55304 | tf_op jit(solution)/shard_map/ppermute | solution.py:23
  6.5 1.4 %copy.41 = f32[3,512,3]{1,2,0:T(4,128)S(1)} copy(f32[3,512,3]{2,1,0:T(8,128)} %get-tuple-element.15) | data formatting | bytes 36864
  7.9 4.8 %collective-permute-start.3 = (f32[3,512,3]{1,2,0:T(4,128)S(1)}, f32[3,512,3]{1,2,0:T(4,128)S(1)}, u32[]{:S(2)}, u32[]{:S(2)}) collective-permute-start(f32[3,512,3]{1,2,0:T(4,128)S(1)} %copy.41), channel_id=1, source_target_pairs={{0,1},{1,2},{2,3},{3,4},{4,5},{5,6},{6,7},{7,8},{8,9},{9,10},{10,1... | collective-permute-start | bytes 55304 | tf_op jit(solution)/shard_map/ppermute | solution.py:21
  12.7 0.0 collective-permute-start.1
  12.7 0.0 copy-done
  12.8 1.5 %multiply_bitcast_fusion = (f32[512,512]{1,0:T(8,128)}, f32[512,512]{1,0:T(8,128)}) fusion(f32[3,512,512]{2,1,0:T(8,128)S(1)} %copy-done), kind=kLoop, calls=%fused_computation.32 | loop fusion | flops 262144 | bytes 4194304 | tf_op jit(solution)/shard_map/mul | solution.py:141
  14.3 0.0 copy-done.7
  14.3 0.0 copy-done.8
  14.3 0.0 copy-done.1
  14.3 0.3 constant_dynamic-update-slice_fusion.1
  14.6 0.0 collective-permute-done
  14.7 0.0 collective-permute-done.2
  14.7 1.2 %copy.26 = f32[3,512,3]{2,1,0:T(8,128)} copy(f32[3,512,3]{1,2,0:T(4,128)S(1)} %collective-permute-done.2) | data formatting | bytes 36864 | tf_op jit(solution)/shard_map/ppermute | solution.py:23
  15.9 0.0 collective-permute-done.3
  15.9 1.2 %copy.28 = f32[3,512,3]{2,1,0:T(8,128)} copy(f32[3,512,3]{1,2,0:T(4,128)S(1)} %collective-permute-done.3) | data formatting | bytes 36864 | tf_op jit(solution)/shard_map/ppermute | solution.py:21
  17.2 0.0 collective-permute-done.1
  17.2 0.0 copy-start.4
  17.2 18.3 %add_multiply_fusion = f32[3,512,512]{2,1,0:T(8,128)S(1)} fusion(f32[3,512,512]{2,1,0:T(8,128)} %param.11, f32[3,512,3]{2,1,0:T(8,128)} %copy.26, f32[3,512,3]{2,1,0:T(8,128)} %copy.28, f32[3,3,512]{2,1,0:T(4,128)S(1)} %collective-permute-done.1, f32[3,515,512]{2,1,0:T(8,128)S(1)} %constant_dynamic-update-slice_fusion, f32[512]{0:T(512)S(1)} %get-tuple-element.25, ...), kind=kLoop, calls=%fused_computation.27 | loop fusion | flops 43253760 | bytes 17887232 | tf_op jit(solution)/shard_map/mul | solution.py:144
  35.4 0.0 copy-done.4
  35.5 0.0 copy-start.5
  35.5 0.0 copy-start.6
  35.5 5.6 %fusion.10 = f32[3,510,512]{2,1,0:T(8,128)S(1)} fusion(f32[510,510,1]{1,0,2:T(8,128)S(1)} %copy-done.4, f32[3,512,512]{2,1,0:T(8,128)S(1)} %add_multiply_fusion), kind=kOutput, calls=%fused_computation.28 | convolution fusion | flops 4794163200 | bytes 7319568 | tf_op jit(solution)/shard_map/cjy,ij->ciy/dot_general | solution.py:113
  41.2 20.5 %all_gather.6 = f32[3,32,512]{2,0,1:T(4,128)S(1)} all-gather(f32[3,2,512]{2,0,1:T(4,128)S(1)} %copy.29), channel_id=1, replica_groups=mesh['gx'=16,'gy'=16] {'gx'}, dimensions={1}, use_global_device_ids=true | all-gather | bytes 208896 | tf_op jit(solution)/shard_map/all_gather | solution.py:118
  61.7 1.0 convolution_bitcast_fusion.1
  62.7 0.0 copy-done.5
  62.7 0.0 copy-done.6
  62.7 0.5 multiply_add_fusion.1
  63.2 0.4 maximum_multiply_fusion
  63.7 5.5 %fusion.6 = f32[3,512,510]{1,2,0:T(8,128)S(1)} fusion(f32[510,510,1]{1,0,2:T(8,128)S(1)} %copy-done.4, f32[3,512,512]{2,1,0:T(8,128)S(1)} %maximum_multiply_fusion), kind=kOutput, calls=%fused_computation.16 | convolution fusion | flops 4794163200 | bytes 7319568 | tf_op jit(solution)/shard_map/cxj,ij->cxi/dot_general | solution.py:150
  69.1 0.0 copy-start.2
  69.1 1.7 %copy-done.2 = f32[3,512,510]{1,2,0:T(8,128)} copy-done((f32[3,512,510]{1,2,0:T(8,128)}, f32[3,512,510]{1,2,0:T(8,128)S(1)}, u32[]{:S(2)}) %copy-start.2) | copy-done | bytes 3133464
  70.8 1.2 %copy.42 = f32[3,512,1]{2,1,0:T(8,128)} copy(f32[3,512,1]{1,2,0:T(1,128)S(1)} %get-tuple-element.10) | data formatting | bytes 12288
  72.0 1.2 %copy.43 = f32[3,512,1]{2,1,0:T(8,128)} copy(f32[3,512,1]{1,2,0:T(1,128)S(1)} %get-tuple-element.9) | data formatting | bytes 12288
  73.2 0.0 copy-start.3
  73.2 2.2 %fusion.14 = (f32[3,512]{1,0:T(4,128)S(1)}, f32[3,512]{1,0:T(4,128)S(1)}) fusion(f32[3,512,512]{2,1,0:T(8,128)S(1)} %maximum_multiply_fusion, f32[3,512,1]{2,1,0:T(8,128)} %copy.42, f32[3,512,1]{2,1,0:T(8,128)} %copy.43), kind=kLoop, calls=%fused_computation.36 | loop fusion | flops 6144 | bytes 36864 | tf_op jit(solution)/shard_map/sub | solution.py:151
  75.5 27.3 %all_gather.7 = f32[3,32,512]{2,0,1:T(4,128)S(1)} all-gather(f32[3,2,512]{2,0,1:T(4,128)S(1)} %copy.33), channel_id=1, replica_groups=mesh['gx'=16,'gy'=16] {'gy'}, dimensions={1}, use_global_device_ids=true | all-gather | bytes 208896 | tf_op jit(solution)/shard_map/all_gather | solution.py:155
  102.9 1.0 convolution_bitcast_fusion
  103.9 0.0 copy-done.3
  103.9 0.5 multiply_add_fusion
  104.5 0.4 pad_maximum_fusion.3
  104.9 2.4 %copy.35 = f32[3,512,512]{2,1,0:T(8,128)} copy(f32[3,512,512]{1,2,0:T(8,128)S(1)} %pad_maximum_fusion.3) | data formatting | bytes 6291456 | tf_op jit(solution)/shard_map/concatenate | solution.py:160
  (17 shorter events, 0.2 us)
Async XLA Ops:
  0.0 12.7 %copy-start = (f32[3,512,512]{2,1,0:T(8,128)S(1)}, f32[3,512,512]{2,1,0:T(8,128)}, u32[]{:S(2)}) copy-start(f32[3,512,512]{2,1,0:T(8,128)} %param.11) | copy-start | bytes 9437188
  1.0 13.7 %collective-permute-start = (f32[3,3,512]{2,1,0:T(4,128)S(1)}, f32[3,3,512]{2,1,0:T(4,128)S(1)}, u32[]{:S(2)}, u32[]{:S(2)}) collective-permute-start(f32[3,3,512]{2,1,0:T(4,128)S(1)} %get-tuple-element.13), channel_id=1, source_target_pairs={{16,0},{32,16},{48,32},{64,48},{80,64},{96,80},{112,96},{128,112},... | collective-permute-start | bytes 55304 | tf_op jit(solution)/shard_map/ppermute | solution.py:23
  3.8 10.5 %copy-start.7 = (f32[512]{0:T(512)S(1)}, f32[512]{0:T(512)}, u32[]{:S(2)}) copy-start(f32[512]{0:T(512)} %param.12) | copy-start | bytes 6148
  3.8 10.5 %copy-start.8 = (f32[512]{0:T(512)S(1)}, f32[512]{0:T(512)}, u32[]{:S(2)}) copy-start(f32[512]{0:T(512)} %param.13) | copy-start | bytes 6148
  5.2 9.5 %collective-permute-start.2 = (f32[3,512,3]{1,2,0:T(4,128)S(1)}, f32[3,512,3]{1,2,0:T(4,128)S(1)}, u32[]{:S(2)}, u32[]{:S(2)}) collective-permute-start(f32[3,512,3]{1,2,0:T(4,128)S(1)} %copy.40), channel_id=1, source_target_pairs={{1,0},{2,1},{3,2},{4,3},{5,4},{6,5},{7,6},{8,7},{9,8},{10,9},{11,1... | collective-permute-start | bytes 55304 | tf_op jit(solution)/shard_map/ppermute | solution.py:23
  7.9 6.4 %copy-start.1 = (f32[3,512,512]{2,1,0:T(8,128)S(1)}, f32[3,512,512]{2,1,0:T(8,128)}, u32[]{:S(2)}) copy-start(f32[3,512,512]{2,1,0:T(8,128)} %param.11) | copy-start | bytes 9437188
  7.9 8.0 %collective-permute-start.3 = (f32[3,512,3]{1,2,0:T(4,128)S(1)}, f32[3,512,3]{1,2,0:T(4,128)S(1)}, u32[]{:S(2)}, u32[]{:S(2)}) collective-permute-start(f32[3,512,3]{1,2,0:T(4,128)S(1)} %copy.41), channel_id=1, source_target_pairs={{0,1},{1,2},{2,3},{3,4},{4,5},{5,6},{6,7},{7,8},{8,9},{9,10},{10,1... | collective-permute-start | bytes 55304 | tf_op jit(solution)/shard_map/ppermute | solution.py:21
  12.7 4.4 %collective-permute-start.1 = (f32[3,3,512]{2,1,0:T(4,128)S(1)}, f32[3,3,512]{2,1,0:T(4,128)S(1)}, u32[]{:S(2)}, u32[]{:S(2)}) collective-permute-start(f32[3,3,512]{2,1,0:T(4,128)S(1)} %get-tuple-element.14), channel_id=1, source_target_pairs={{0,16},{16,32},{32,48},{48,64},{64,80},{80,96},{96,112},{112,128},... | collective-permute-start | bytes 55304 | tf_op jit(solution)/shard_map/ppermute | solution.py:21
  17.2 18.3 %copy-start.4 = (f32[510,510,1]{1,0,2:T(8,128)S(1)}, f32[510,510,1]{1,0,2:T(8,128)}, u32[]{:S(2)}) copy-start(f32[510,510,1]{1,0,2:T(8,128)} %constant.59) | copy-start | bytes 3121204
  35.5 27.2 %copy-start.5 = (f32[510]{0:T(512)S(1)}, f32[510]{0:T(512)}, u32[]{:S(2)}) copy-start(f32[510]{0:T(512)} %constant.56.clone) | copy-start | bytes 6124
  35.5 27.2 %copy-start.6 = (f32[510]{0:T(512)S(1)}, f32[510]{0:T(512)}, u32[]{:S(2)}) copy-start(f32[510]{0:T(512)} %constant.57.clone) | copy-start | bytes 6124
  69.1 1.7 %copy-start.2 = (f32[3,512,510]{1,2,0:T(8,128)}, f32[3,512,510]{1,2,0:T(8,128)S(1)}, u32[]{:S(2)}) copy-start(f32[3,512,510]{1,2,0:T(8,128)S(1)} %fusion.6) | copy-start | bytes 9400324
  73.2 30.6 %copy-start.3 = (f32[3,512,510]{1,2,0:T(8,128)S(1)}, f32[3,512,510]{1,2,0:T(8,128)}, u32[]{:S(2)}) copy-start(f32[3,512,510]{1,2,0:T(8,128)} %copy-done.2) | copy-start | bytes 9400324
where the time goes:
time: 108 us; the launch traced here: 107 us
  blocking collectives  47.8 us (44%)
  other arithmetic  24 us (22%)
  local copies, waits for them, and re-layouts  15.9 us (15%)
  matrix products  13 us (12%)
  starting transfers between devices  6.14 us (6%)
    all_gather x1, blocking collectives, local(): lax.all_gather(ends, 'gy', axis=1, tiled=True)  27.3 us
    all_gather x1, blocking collectives, partitioned_x(): lax.all_gather(ends, 'gx', axis=1, tiled=True)  20.5 us
    mul x1, other arithmetic, local(): right_side = tendency * (math.sqrt(sig_x * sig_y) / diag_x)  18.3 us
    unnamed x27, local copies, waits for them, and re-layouts  7.26 us
    dot_general x1, matrix products, partitioned_x(): jnp.einsum('cjy,ij->ciy', right_side[:, 1:-1, :], inverse, precision=HIGH...  5.63 us
    dot_general x1, matrix products, local(): jnp.einsum('cxj,ij->cxi', y_lines[..., 1:-1], inverse, precision=HIGHEST)  5.46 us
    ppermute x2, starting transfers between devices, extended(): lax.ppermute(tail, axis, [(i, (i + 1) % count) for i in range(ends)])  4.83 us
    slice x1, local copies, waits for them, and re-layouts, extended(): lax.slice_in_dim(cells, cells.shape[dim] - width, cells.shape[dim], axis=...  2.76 us
  transfers between devices with their start and end apart: 4, of which 0 were waited for; matrix products, arithmetic and copies ran while one was open for 9% of the time, Pallas kernels for 0%

commit v1 on v0

--- a/solution.py
+++ b/solution.py
@@ -152,7 +152,11 @@
     tail_val = y_lines[..., -1] - low_y * interior[..., -1]
     ends = jnp.stack([head_val, tail_val], axis=1)
     solved = make_fold(
-        own_rows, jnp.zeros(ends.shape, jnp.float32), lax.all_gather(ends, "gy", axis=1, tiled=True)
+        own_rows,
+        jnp.zeros(ends.shape, jnp.float32),
+        jnp.concatenate(
+            lax.all_to_all(jnp.stack([ends] * lax.axis_size("gy")), "gy", 0, 0), axis=1
+        ),
     )
     head_y = solved[:, 0][..., None]
     tail_y = solved[:, 1][..., None]

time: 108 us -> 101 us (0.935)
  blocking collectives: 47.8 us -> 20.5 us
  starting transfers between devices: 6.14 us -> 15.1 us
  waiting for transfers between devices: 0.01 us -> 8.36 us
  other arithmetic: 24 us -> 25.8 us
    all_gather x1 -> x0, blocking collectives: 27.3 us -> none  [local(): lax.all_gather(ends, 'gy', axis=1, tiled=True)]
    all_to_all x0 -> x1, starting transfers between devices: none -> 8.97 us  [local(): lax.all_to_all(jnp.stack([ends] * lax.axis_size('gy')), 'gy', 0, 0)]
    all_to_all x0 -> x1, waiting for transfers between devices: none -> 8.35 us  [local(): lax.all_to_all(jnp.stack([ends] * lax.axis_size('gy')), 'gy', 0, 0)]
    add x1, other arithmetic: 0.55 us -> 2.43 us  [local(): middle = interior + head_col * head_y + tail_col * tail_y]
    unnamed x27 -> x25, local copies, waits for them, and re-layouts: 7.26 us -> 7.25 us
  transfers between devices with their start and end apart: 4 -> 5, of which waited for: 0 -> 1; matrix products, arithmetic and copies ran while one was open for 9% -> 10% of each run, Pallas kernels for 0% -> 0%
where the time goes in v1:
time: 101 us; the launch traced here: 99.8 us
  other arithmetic  25.8 us (26%)
  blocking collectives  20.5 us (20%)
  local copies, waits for them, and re-layouts  16.7 us (17%)
  starting transfers between devices  15.1 us (15%)
  matrix products  12.9 us (13%)
  waiting for transfers between devices  8.36 us (8%)
    all_gather x1, blocking collectives, partitioned_x(): lax.all_gather(ends, 'gx', axis=1, tiled=True)  20.5 us
    mul x1, other arithmetic, local(): right_side = tendency * (math.sqrt(sig_x * sig_y) / diag_x)  18.3 us
    all_to_all x1, starting transfers between devices, local(): lax.all_to_all(jnp.stack([ends] * lax.axis_size('gy')), 'gy', 0, 0)  8.97 us
    all_to_all x1, waiting for transfers between devices, local(): lax.all_to_all(jnp.stack([ends] * lax.axis_size('gy')), 'gy', 0, 0)  8.35 us
    unnamed x25, local copies, waits for them, and re-layouts  7.25 us
    dot_general x1, matrix products, partitioned_x(): jnp.einsum('cjy,ij->ciy', right_side[:, 1:-1, :], inverse, precision=HIGH...  5.62 us
    dot_general x1, matrix products, local(): jnp.einsum('cxj,ij->cxi', y_lines[..., 1:-1], inverse, precision=HIGHEST)  5.46 us
    ppermute x2, starting transfers between devices, extended(): lax.ppermute(tail, axis, [(i, (i + 1) % count) for i in range(ends)])  4.83 us
  transfers between devices with their start and end apart: 5, of which 1 were waited for; matrix products, arithmetic and copies ran while one was open for 10% of the time, Pallas kernels for 0%

profile of v1, /device:TPU:32, one launch (start us, length us, event | category | flops | bytes accessed | tf_op | source)
XLA Modules:
  0.0 99.8 jit_solution(3380639758905340918)
XLA Ops:
  0.0 0.0 copy-start
  0.0 1.0 fusion.25
  1.0 0.0 collective-permute-start
  1.0 2.8 %fusion.26 = (f32[3,512,3]{2,1,0:T(8,128)}, f32[3,512,3]{2,1,0:T(8,128)}) fusion(f32[3,512,512]{2,1,0:T(8,128)} %param.11), kind=kLoop, calls=%fused_computation.63 | loop fusion | bytes 73728 | tf_op jit(solution)/shard_map/slice | solution.py:18
  3.8 0.0 copy-start.6
  3.8 0.0 copy-start.7
  3.8 1.4 %copy.39 = f32[3,512,3]{1,2,0:T(4,128)S(1)} copy(f32[3,512,3]{2,1,0:T(8,128)} %get-tuple-element.16) | data formatting | bytes 36864
  5.2 1.3 %collective-permute-start.2 = (f32[3,512,3]{1,2,0:T(4,128)S(1)}, f32[3,512,3]{1,2,0:T(4,128)S(1)}, u32[]{:S(2)}, u32[]{:S(2)}) collective-permute-start(f32[3,512,3]{1,2,0:T(4,128)S(1)} %copy.39), channel_id=1, source_target_pairs={{1,0},{2,1},{3,2},{4,3},{5,4},{6,5},{7,6},{8,7},{9,8},{10,9},{11,1... | collective-permute-start | bytes 55304 | tf_op jit(solution)/shard_map/ppermute | solution.py:23
  6.5 1.4 %copy.40 = f32[3,512,3]{1,2,0:T(4,128)S(1)} copy(f32[3,512,3]{2,1,0:T(8,128)} %get-tuple-element.15) | data formatting | bytes 36864
  7.9 4.8 %collective-permute-start.3 = (f32[3,512,3]{1,2,0:T(4,128)S(1)}, f32[3,512,3]{1,2,0:T(4,128)S(1)}, u32[]{:S(2)}, u32[]{:S(2)}) collective-permute-start(f32[3,512,3]{1,2,0:T(4,128)S(1)} %copy.40), channel_id=1, source_target_pairs={{0,1},{1,2},{2,3},{3,4},{4,5},{5,6},{6,7},{7,8},{8,9},{9,10},{10,1... | collective-permute-start | bytes 55304 | tf_op jit(solution)/shard_map/ppermute | solution.py:21
  12.7 0.0 collective-permute-start.1
  12.7 0.0 copy-done
  12.8 1.5 %multiply_bitcast_fusion = (f32[512,512]{1,0:T(8,128)}, f32[512,512]{1,0:T(8,128)}) fusion(f32[3,512,512]{2,1,0:T(8,128)S(1)} %copy-done), kind=kLoop, calls=%fused_computation.32 | loop fusion | flops 262144 | bytes 4194304 | tf_op jit(solution)/shard_map/mul | solution.py:141
  14.3 0.0 copy-done.6
  14.3 0.0 copy-done.7
  14.3 0.0 copy-done.1
  14.3 0.3 constant_dynamic-update-slice_fusion.1
  14.6 0.0 collective-permute-done
  14.7 0.0 collective-permute-done.2
  14.7 1.2 %copy.26 = f32[3,512,3]{2,1,0:T(8,128)} copy(f32[3,512,3]{1,2,0:T(4,128)S(1)} %collective-permute-done.2) | data formatting | bytes 36864 | tf_op jit(solution)/shard_map/ppermute | solution.py:23
  15.9 0.0 collective-permute-done.3
  15.9 1.2 %copy.28 = f32[3,512,3]{2,1,0:T(8,128)} copy(f32[3,512,3]{1,2,0:T(4,128)S(1)} %collective-permute-done.3) | data formatting | bytes 36864 | tf_op jit(solution)/shard_map/ppermute | solution.py:21
  17.1 0.0 collective-permute-done.1
  17.1 18.3 %add_multiply_fusion = f32[3,512,512]{2,1,0:T(8,128)S(1)} fusion(f32[3,512,512]{2,1,0:T(8,128)} %param.11, f32[3,512,3]{2,1,0:T(8,128)} %copy.26, f32[3,512,3]{2,1,0:T(8,128)} %copy.28, f32[3,3,512]{2,1,0:T(4,128)S(1)} %collective-permute-done.1, f32[3,515,512]{2,1,0:T(8,128)S(1)} %constant_dynamic-update-slice_fusion, f32[512]{0:T(512)S(1)} %get-tuple-element.25, ...), kind=kLoop, calls=%fused_computation.27 | loop fusion | flops 43253760 | bytes 17887232 | tf_op jit(solution)/shard_map/mul | solution.py:144
  35.5 0.0 copy-done.3
  35.5 0.0 copy-start.4
  35.5 0.0 copy-start.5
  35.5 5.6 %fusion.10 = f32[3,510,512]{2,1,0:T(8,128)S(1)} fusion(f32[510,510,1]{1,0,2:T(8,128)S(1)} %copy-done.3, f32[3,512,512]{2,1,0:T(8,128)S(1)} %add_multiply_fusion), kind=kOutput, calls=%fused_computation.28 | convolution fusion | flops 4794163200 | bytes 7319568 | tf_op jit(solution)/shard_map/cjy,ij->ciy/dot_general | solution.py:113
  41.2 20.5 %all_gather.3 = f32[3,32,512]{2,0,1:T(4,128)S(1)} all-gather(f32[3,2,512]{2,0,1:T(4,128)S(1)} %copy.29), channel_id=1, replica_groups=mesh['gx'=16,'gy'=16] {'gx'}, dimensions={1}, use_global_device_ids=true | all-gather | bytes 208896 | tf_op jit(solution)/shard_map/all_gather | solution.py:118
  61.7 1.0 convolution_bitcast_fusion.1
  62.7 0.0 copy-done.4
  62.7 0.0 copy-done.5
  62.7 0.5 multiply_add_fusion.1
  63.3 0.4 maximum_multiply_fusion
  63.7 5.5 %fusion.6 = f32[3,512,510]{1,2,0:T(8,128)S(1)} fusion(f32[510,510,1]{1,0,2:T(8,128)S(1)} %copy-done.3, f32[3,512,512]{2,1,0:T(8,128)S(1)} %maximum_multiply_fusion), kind=kOutput, calls=%fused_computation.16 | convolution fusion | flops 4794163200 | bytes 7319568 | tf_op jit(solution)/shard_map/cxj,ij->cxi/dot_general | solution.py:150
  69.2 0.0 copy-start.2
  69.2 1.7 %copy-done.2 = f32[3,512,510]{1,2,0:T(8,128)} copy-done((f32[3,512,510]{1,2,0:T(8,128)}, f32[3,512,510]{1,2,0:T(8,128)S(1)}, u32[]{:S(2)}) %copy-start.2) | copy-done | bytes 3133464
  70.9 1.2 %copy.41 = f32[3,512,1]{2,1,0:T(8,128)} copy(f32[3,512,1]{1,2,0:T(1,128)S(1)} %get-tuple-element.10) | data formatting | bytes 12288
  72.1 1.2 %copy.42 = f32[3,512,1]{2,1,0:T(8,128)} copy(f32[3,512,1]{1,2,0:T(1,128)S(1)} %get-tuple-element.9) | data formatting | bytes 12288
  73.3 2.1 %fusion.14 = (f32[3,512]{1,0:T(4,128)S(1)}, f32[3,512]{1,0:T(4,128)S(1)}) fusion(f32[3,512,512]{2,1,0:T(8,128)S(1)} %maximum_multiply_fusion, f32[3,512,1]{2,1,0:T(8,128)} %copy.41, f32[3,512,1]{2,1,0:T(8,128)} %copy.42), kind=kLoop, calls=%fused_computation.36 | loop fusion | flops 6144 | bytes 36864 | tf_op jit(solution)/shard_map/sub | solution.py:151
  75.4 0.7 stack.8
  76.1 9.0 %all-to-all-start = ((f32[16,3,2,512]{3,2,1,0:T(2,128)}), f32[16,3,2,512]{3,2,1,0:T(2,128)S(1)}, u32[]{:S(2)}, u32[]{:S(2)}) async-start(f32[16,3,2,512]{3,2,1,0:T(2,128)} %stack.8), calls=%async_computation | async-start | bytes 393216 | tf_op jit(solution)/shard_map/all_to_all | solution.py:158
  85.1 8.4 %all-to-all-done = f32[16,3,2,512]{3,2,1,0:T(2,128)S(1)} async-done(((f32[16,3,2,512]{3,2,1,0:T(2,128)}), f32[16,3,2,512]{3,2,1,0:T(2,128)S(1)}, u32[]{:S(2)}, u32[]{:S(2)}) %all-to-all-start) | async-done | bytes 196640 | tf_op jit(solution)/shard_map/all_to_all | solution.py:158
  93.5 0.1 reshape.66
  93.6 0.9 convolution_bitcast_fusion
  94.6 2.4 %multiply_add_fusion = f32[3,512,510]{1,2,0:T(8,128)S(1)} fusion(f32[3,512,510]{1,2,0:T(8,128)} %copy-done.2, f32[3,512]{1,0:T(4,128)S(1)} %bitcast.38, f32[510]{0:T(512)S(1)} %copy-done.5, f32[3,512]{1,0:T(4,128)S(1)} %bitcast.39, f32[510]{0:T(512)S(1)} %copy-done.4), kind=kLoop, calls=%fused_computation.25 | loop fusion | flops 3133440 | bytes 6283248 | tf_op jit(solution)/shard_map/add | solution.py:163
  97.0 0.4 pad_maximum_fusion.3
  97.5 2.4 %copy.34 = f32[3,512,512]{2,1,0:T(8,128)} copy(f32[3,512,512]{1,2,0:T(8,128)S(1)} %pad_maximum_fusion.3) | data formatting | bytes 6291456 | tf_op jit(solution)/shard_map/concatenate | solution.py:164
  (18 shorter events, 0.2 us)
Async XLA Ops:
  0.0 12.7 %copy-start = (f32[3,512,512]{2,1,0:T(8,128)S(1)}, f32[3,512,512]{2,1,0:T(8,128)}, u32[]{:S(2)}) copy-start(f32[3,512,512]{2,1,0:T(8,128)} %param.11) | copy-start | bytes 9437188
  1.0 13.7 %collective-permute-start = (f32[3,3,512]{2,1,0:T(4,128)S(1)}, f32[3,3,512]{2,1,0:T(4,128)S(1)}, u32[]{:S(2)}, u32[]{:S(2)}) collective-permute-start(f32[3,3,512]{2,1,0:T(4,128)S(1)} %get-tuple-element.13), channel_id=1, source_target_pairs={{16,0},{32,16},{48,32},{64,48},{80,64},{96,80},{112,96},{128,112},... | collective-permute-start | bytes 55304 | tf_op jit(solution)/shard_map/ppermute | solution.py:23
  3.8 10.5 %copy-start.6 = (f32[512]{0:T(512)S(1)}, f32[512]{0:T(512)}, u32[]{:S(2)}) copy-start(f32[512]{0:T(512)} %param.12) | copy-start | bytes 6148
  3.8 10.5 %copy-start.7 = (f32[512]{0:T(512)S(1)}, f32[512]{0:T(512)}, u32[]{:S(2)}) copy-start(f32[512]{0:T(512)} %param.13) | copy-start | bytes 6148
  5.2 9.5 %collective-permute-start.2 = (f32[3,512,3]{1,2,0:T(4,128)S(1)}, f32[3,512,3]{1,2,0:T(4,128)S(1)}, u32[]{:S(2)}, u32[]{:S(2)}) collective-permute-start(f32[3,512,3]{1,2,0:T(4,128)S(1)} %copy.39), channel_id=1, source_target_pairs={{1,0},{2,1},{3,2},{4,3},{5,4},{6,5},{7,6},{8,7},{9,8},{10,9},{11,1... | collective-permute-start | bytes 55304 | tf_op jit(solution)/shard_map/ppermute | solution.py:23
  7.9 6.4 %copy-start.1 = (f32[3,512,512]{2,1,0:T(8,128)S(1)}, f32[3,512,512]{2,1,0:T(8,128)}, u32[]{:S(2)}) copy-start(f32[3,512,512]{2,1,0:T(8,128)} %param.11) | copy-start | bytes 9437188
  7.9 8.0 %collective-permute-start.3 = (f32[3,512,3]{1,2,0:T(4,128)S(1)}, f32[3,512,3]{1,2,0:T(4,128)S(1)}, u32[]{:S(2)}, u32[]{:S(2)}) collective-permute-start(f32[3,512,3]{1,2,0:T(4,128)S(1)} %copy.40), channel_id=1, source_target_pairs={{0,1},{1,2},{2,3},{3,4},{4,5},{5,6},{6,7},{7,8},{8,9},{9,10},{10,1... | collective-permute-start | bytes 55304 | tf_op jit(solution)/shard_map/ppermute | solution.py:21
  12.7 4.4 %collective-permute-start.1 = (f32[3,3,512]{2,1,0:T(4,128)S(1)}, f32[3,3,512]{2,1,0:T(4,128)S(1)}, u32[]{:S(2)}, u32[]{:S(2)}) collective-permute-start(f32[3,3,512]{2,1,0:T(4,128)S(1)} %get-tuple-element.14), channel_id=1, source_target_pairs={{0,16},{16,32},{32,48},{48,64},{64,80},{80,96},{96,112},{112,128},... | collective-permute-start | bytes 55304 | tf_op jit(solution)/shard_map/ppermute | solution.py:21
  17.1 18.4 %copy-start.3 = (f32[510,510,1]{1,0,2:T(8,128)S(1)}, f32[510,510,1]{1,0,2:T(8,128)}, u32[]{:S(2)}) copy-start(f32[510,510,1]{1,0,2:T(8,128)} %constant.59) | copy-start | bytes 3121204
  35.5 27.2 %copy-start.4 = (f32[510]{0:T(512)S(1)}, f32[510]{0:T(512)}, u32[]{:S(2)}) copy-start(f32[510]{0:T(512)} %constant.56.clone) | copy-start | bytes 6124
  35.5 27.2 %copy-start.5 = (f32[510]{0:T(512)S(1)}, f32[510]{0:T(512)}, u32[]{:S(2)}) copy-start(f32[510]{0:T(512)} %constant.57.clone) | copy-start | bytes 6124
  69.2 1.7 %copy-start.2 = (f32[3,512,510]{1,2,0:T(8,128)}, f32[3,512,510]{1,2,0:T(8,128)S(1)}, u32[]{:S(2)}) copy-start(f32[3,512,510]{1,2,0:T(8,128)S(1)} %fusion.6) | copy-start | bytes 9400324
  76.1 17.3 %all-to-all-start = ((f32[16,3,2,512]{3,2,1,0:T(2,128)}), f32[16,3,2,512]{3,2,1,0:T(2,128)S(1)}, u32[]{:S(2)}, u32[]{:S(2)}) async-start(f32[16,3,2,512]{3,2,1,0:T(2,128)} %stack.8), calls=%async_computation | async-start | bytes 393216 | tf_op jit(solution)/shard_map/all_to_all | solution.py:158
